TPU v7x, 32 devices: a whole 2x2x4 slice. The times are simulated.
32 devices in a mesh: section: 8 (over y, x, core), rep: 4 (over z).
Axes of the slice: x: 2, y: 2, z: 4, core: 2. Of those that a mesh axis runs over, the one named last changes fastest.
Arguments:
- inflow: bfloat16 [8, 4, 4, 16, 3584], P('section', 'rep'), may hold values from -6 to 6
- cotangent: bfloat16 [8, 4, 4, 16, 3584], P('section', 'rep'), may hold values from -0.1796875 to 0.1796875
- reduce_weight: bfloat16 [8, 4, 3584, 192], P('section', 'rep'), may hold values from -0.09375 to 0.09375
- expand_weight: bfloat16 [8, 4, 3584, 192], P('section', 'rep'), may hold values from -0.4375 to 0.4375
- held: int32 [8, 4], replicated, may hold values from 0 to 4, as said below
- routes: int32 [2, 8, 4, 4], replicated, may hold values from 0 to 3, as said below
Outputs:
- reduce_grad: bfloat16 [8, 3584, 192], P('section', 'rep')
- expand_grad: bfloat16 [8, 3584, 192], P('section', 'rep')
Inputs may be any that keep to these rules, and one draw needn't show every extreme that they name: Lanes of a device at the first tick sit in slots 0 to held - 1. Sections above 5 hold none; every other section has a replica that holds 4. `routes`: within one section and tick the 4 slots of a device name distinct replicas, and every replica is named by exactly 4 slots of the section, live or not.
All inputs are finite; a program needn't handle non-finite values.
Results may differ from a plain program's by a relative error of at most 0.014.
Values may be sent and summed in bfloat16 or wider, within the bound.
A program may use at most 64 MiB of HBM per device.

v0:
```python
import jax
import jax.numpy as jnp
from jax import lax
from jax.sharding import PartitionSpec as P

TICKS = 3


epsilon = 1e-06


def from_behind(block, axis, distance):
    devices = range(lax.axis_size(axis))
    route = [(i - distance, i) for i in devices if i - distance in devices]
    return lax.ppermute(block, axis, route)


def wiring(counts, targets, replicas, capacity):
    slot_ids = jnp.arange(capacity, dtype=jnp.int32)
    replica_ids = jnp.arange(replicas, dtype=jnp.int32)
    slot_live = slot_ids[None, None, :] < counts[:, :, None]
    matched = (
        slot_live[:, :, :, None] & (targets[:, :, :, None] == replica_ids[None, None, None, :])
    ).astype(jnp.int32)
    pair_sent = jnp.sum(matched, axis=2)
    pair_slot = jnp.sum(matched * slot_ids[None, None, :, None], axis=2)
    pair_rank = jnp.cumsum(pair_sent, axis=1) - pair_sent
    arrived = jnp.sum(pair_sent, axis=1)
    following = jnp.concatenate([jnp.zeros_like(arrived[:1]), arrived[:-1]], axis=0)
    return (slot_live, pair_sent, pair_slot, pair_rank, following)


def gather_slots(source, slot_index, present):
    picked = jnp.take(source, slot_index, axis=0)
    return jnp.where(present[:, None, None], picked, jnp.zeros_like(picked))


def compact(received, sent_column, rank_column, capacity):
    slot_ids = jnp.arange(capacity, dtype=jnp.int32)
    source_ids = jnp.arange(received.shape[0], dtype=jnp.int32)
    chosen = ((sent_column[:, None] == 1) & (rank_column[:, None] == slot_ids[None, :])).astype(
        jnp.int32
    )
    source_rep = jnp.sum(chosen * source_ids[:, None], axis=0)
    present = jnp.sum(chosen, axis=0) == 1
    return gather_slots(received, source_rep, present)


def layer_parts(current, reduce_w):
    flat_rows = current.reshape(-1, current.shape[-1])
    widened = flat_rows.astype(jnp.float32)
    inverse_rms = lax.rsqrt(jnp.mean(widened * widened, axis=-1, keepdims=True) + epsilon)
    unit_rows = widened * inverse_rms
    normed = unit_rows.astype(jnp.bfloat16)
    pre_act = jnp.dot(normed, reduce_w, preferred_element_type=jnp.float32)
    hidden = jax.nn.silu(pre_act).astype(jnp.bfloat16)
    return (widened, inverse_rms, unit_rows, normed, pre_act, hidden)


def onward(outputs, table, section_id, replica_id):
    slot_live, pair_sent, pair_slot, pair_rank = table
    capacity = outputs.shape[0]
    shifted = from_behind(outputs, "section", 1)
    source_section = jnp.maximum(section_id - 1, 0)
    bucket = gather_slots(
        shifted, pair_slot[source_section, replica_id], pair_sent[source_section, replica_id] == 1
    )
    received = lax.all_to_all(bucket, "rep", split_axis=0, concat_axis=0, tiled=True)
    return compact(
        received,
        pair_sent[source_section, :, replica_id],
        pair_rank[source_section, :, replica_id],
        capacity,
    )


def homeward(returned, table, targets, section_id, replica_id):
    slot_live, pair_sent, pair_slot, pair_rank = table
    source_section = jnp.maximum(section_id - 1, 0)
    parcel = gather_slots(
        returned,
        pair_rank[source_section, :, replica_id],
        pair_sent[source_section, :, replica_id] == 1,
    )
    received = lax.all_to_all(parcel, "rep", split_axis=0, concat_axis=0, tiled=True)
    placed = gather_slots(
        received, targets[source_section, replica_id], slot_live[source_section, replica_id]
    )
    return from_behind(placed, "section", -1)


def local(inflow, cotangent, reduce_weight, expand_weight, held, routes):
    section_id = lax.axis_index("section")
    replica_id = lax.axis_index("rep")
    replicas = lax.axis_size("rep")
    capacity = inflow.shape[2]
    feature_count = inflow.shape[4]
    reduce_w = reduce_weight[0, 0]
    expand_w = expand_weight[0, 0]
    bottleneck = reduce_w.shape[1]
    slot_ids = jnp.arange(capacity, dtype=jnp.int32)
    counts = held
    wirings = []
    for step_index in range(TICKS - 1):
        slot_live, pair_sent, pair_slot, pair_rank, counts = wiring(
            counts, routes[step_index], replicas, capacity
        )
        wirings.append((slot_live, pair_sent, pair_slot, pair_rank))
    first_live = slot_ids < held[section_id, replica_id]
    last_live = slot_ids < counts[section_id, replica_id]
    current = jnp.where(first_live[:, None, None], inflow[0, 0], jnp.zeros_like(inflow[0, 0]))
    stashed = []
    contract_last = (((1,), (1,)), ((), ()))
    for step_index in range(TICKS):
        layer_state = layer_parts(current, reduce_w)
        stashed.append(layer_state)
        if step_index < TICKS - 1:
            branch_out = lax.dot_general(
                layer_state[5], expand_w, contract_last, preferred_element_type=jnp.float32
            )
            outputs = (layer_state[0] + branch_out).astype(jnp.bfloat16).reshape(current.shape)
            current = onward(outputs, wirings[step_index], section_id, replica_id)
    upstream = jnp.where(last_live[:, None, None], cotangent[0, 0], jnp.zeros_like(cotangent[0, 0]))
    normed_list = []
    grad_list = []
    upstream_list = []
    hidden_list = []
    for step_index in range(TICKS - 1, -1, -1):
        widened, inverse_rms, unit_rows, normed, pre_act, hidden = stashed[step_index]
        flat_up = upstream.reshape(-1, feature_count)
        grad_hidden = jnp.dot(flat_up, expand_w, preferred_element_type=jnp.float32)
        sigmoid_pre = jax.nn.sigmoid(pre_act)
        grad_pre = (grad_hidden * sigmoid_pre * (1.0 + pre_act * (1.0 - sigmoid_pre))).astype(
            jnp.bfloat16
        )
        normed_list.append(normed)
        grad_list.append(grad_pre)
        upstream_list.append(flat_up)
        hidden_list.append(hidden)
        if step_index > 0:
            grad_unit = lax.dot_general(
                grad_pre, reduce_w, contract_last, preferred_element_type=jnp.float32
            )
            inner_term = jnp.mean(grad_unit * unit_rows, axis=-1, keepdims=True)
            returned = flat_up.astype(jnp.float32) + inverse_rms * (
                grad_unit - unit_rows * inner_term
            )
            returned = returned.astype(jnp.bfloat16).reshape(upstream.shape)
            upstream = homeward(
                returned, wirings[step_index - 1], routes[step_index - 1], section_id, replica_id
            )
    normed_all = jnp.concatenate(normed_list, axis=0)
    grad_all = jnp.concatenate(grad_list, axis=0)
    upstream_all = jnp.concatenate(upstream_list, axis=0)
    hidden_all = jnp.concatenate(hidden_list, axis=0)
    contract_rows = (((0,), (0,)), ((), ()))
    row_share = feature_count // replicas
    reduce_rows = lax.dot_general(
        normed_all, grad_all, contract_rows, preferred_element_type=jnp.float32
    )
    expand_rows = lax.dot_general(
        upstream_all, hidden_all, contract_rows, preferred_element_type=jnp.float32
    )
    summed_all = lax.psum(
        jnp.concatenate([reduce_rows, expand_rows], axis=1).astype(jnp.bfloat16), "rep"
    ).astype(jnp.float32)
    owned = lax.dynamic_slice_in_dim(summed_all, replica_id * row_share, row_share, 0)
    reduce_grad = owned[:, :bottleneck].astype(jnp.bfloat16)[None]
    expand_grad = owned[:, bottleneck:].astype(jnp.bfloat16)[None]
    return (reduce_grad, expand_grad)


def solution(mesh):
    placed = (
        P("section", "rep", None, None, None),
        P("section", "rep", None, None, None),
        P("section", "rep", None, None),
        P("section", "rep", None, None),
        P(),
        P(),
    )
    return jax.shard_map(
        local,
        mesh=mesh,
        in_specs=placed,
        out_specs=(P("section", "rep", None), P("section", "rep", None)),
        check_vma=False,
    )
```

profile of v0, /device:TPU:18, one launch (start us, length us, event | category | flops | bytes accessed | tf_op | source)
XLA Modules:
  0.0 280.2 jit_solution(8124239205391112361)
XLA Ops:
  7.2 1.4 dynamic_slice.55
  8.6 0.6 iota_compare_fusion.7
  9.2 1.3 fusion.58
  10.6 2.1 fusion.59
  12.8 1.7 multiply_convert_fusion.4
  14.5 1.0 fusion.57
  15.5 0.4 fusion
  15.9 1.9 collective-permute-start
  18.3 0.2 compare_reduce_fusion
  18.9 0.2 compare_reduce_fusion.1
  19.2 0.2 fusion.83
  20.3 5.5 %collective-permute-done = bf16[4,16,3584]{2,1,0:T(8,128)(2,1)} collective-permute-done((bf16[4,16,3584]{2,1,0:T(8,128)(2,1)S(1)}, bf16[4,16,3584]{2,1,0:T(8,128)(2,1)}, u32[]{:S(2)}, u32[]{:S(2)}) %collective-permute-start) | collective-permute-done | bytes 458784 | tf_op jit(solution)/shard_map/ppermute | solution.py:15
  25.8 1.6 gather_fusion
  27.4 0.9 select_select_fusion.7
  28.3 5.2 %all-to-all-start = ((bf16[4,16,3584]{2,1,0:T(8,128)(2,1)}), bf16[4,16,3584]{2,1,0:T(8,128)(2,1)}, u32[]{:S(2)}, u32[]{:S(2)}) async-start(bf16[4,16,3584]{2,1,0:T(8,128)(2,1)} %select_select_fusion.7), calls=%async_computation | async-start | bytes 917504 | tf_op jit(solution)/shard_map/all_to_all | solution.py:68
  33.5 0.6 pad_dynamic-slice_fusion
  34.1 8.4 %all-to-all-done = bf16[4,16,3584]{2,1,0:T(8,128)(2,1)} async-done(((bf16[4,16,3584]{2,1,0:T(8,128)(2,1)}), bf16[4,16,3584]{2,1,0:T(8,128)(2,1)}, u32[]{:S(2)}, u32[]{:S(2)}) %all-to-all-start) | async-done | bytes 458784 | tf_op jit(solution)/shard_map/all_to_all | solution.py:68
  42.5 1.6 gather_fusion.1
  44.1 0.3 multiply_reduce_fusion.3
  44.7 0.6 multiply_convert_fusion.3
  45.3 1.1 fusion.1
  46.5 1.9 collective-permute-start.1
  48.4 0.7 iota_compare_fusion.6
  49.4 7.2 %collective-permute-done.1 = bf16[4,16,3584]{2,1,0:T(8,128)(2,1)} collective-permute-done((bf16[4,16,3584]{2,1,0:T(8,128)(2,1)}, bf16[4,16,3584]{2,1,0:T(8,128)(2,1)}, u32[]{:S(2)}, u32[]{:S(2)}) %collective-permute-start.1) | collective-permute-done | bytes 458784 | tf_op jit(solution)/shard_map/ppermute | solution.py:15
  56.6 2.4 gather_fusion.2
  59.0 1.9 select_select_fusion.5
  60.9 7.5 %all-to-all-start.1 = ((bf16[4,16,3584]{2,1,0:T(8,128)(2,1)}), bf16[4,16,3584]{2,1,0:T(8,128)(2,1)}, u32[]{:S(2)}, u32[]{:S(2)}) async-start(bf16[4,16,3584]{2,1,0:T(8,128)(2,1)} %select_select_fusion.5), calls=%async_computation.1 | async-start | bytes 917504 | tf_op jit(solution)/shard_map/all_to_all | solution.py:68
  68.4 1.9 broadcast_select_fusion
  70.3 7.5 %all-to-all-done.1 = bf16[4,16,3584]{2,1,0:T(8,128)(2,1)} async-done(((bf16[4,16,3584]{2,1,0:T(8,128)(2,1)}), bf16[4,16,3584]{2,1,0:T(8,128)(2,1)}, u32[]{:S(2)}, u32[]{:S(2)}) %all-to-all-start.1) | async-done | bytes 458784 | tf_op jit(solution)/shard_map/all_to_all | solution.py:68
  77.8 2.4 gather_fusion.3
  80.2 1.3 multiply_reduce_fusion.2
  81.6 1.3 multiply_convert_fusion
  82.9 0.6 multiply_convert_fusion.2
  83.5 0.6 fusion.54
  84.0 0.4 copy-done.2
  84.5 0.5 multiply_reduce_fusion.1
  85.0 0.5 copy-done.4
  85.5 1.5 add_convert_fusion.1
  87.0 2.4 gather_fusion.4
  89.3 1.9 select_select_fusion.3
  91.2 7.5 %all-to-all-start.2 = ((bf16[4,16,3584]{2,1,0:T(8,128)(2,1)}), bf16[4,16,3584]{2,1,0:T(8,128)(2,1)}, u32[]{:S(2)}, u32[]{:S(2)}) async-start(bf16[4,16,3584]{2,1,0:T(8,128)(2,1)} %select_select_fusion.3), calls=%async_computation.2 | async-start | bytes 917504 | tf_op jit(solution)/shard_map/all_to_all | solution.py:85
  99.0 9.1 %all-to-all-done.2 = bf16[4,16,3584]{2,1,0:T(8,128)(2,1)} async-done(((bf16[4,16,3584]{2,1,0:T(8,128)(2,1)}), bf16[4,16,3584]{2,1,0:T(8,128)(2,1)}, u32[]{:S(2)}, u32[]{:S(2)}) %all-to-all-start.2) | async-done | bytes 458784 | tf_op jit(solution)/shard_map/all_to_all | solution.py:85
  108.0 2.4 gather_fusion.5
  110.4 1.9 select_select_fusion.2
  112.3 1.9 collective-permute-start.2
  114.3 6.2 %collective-permute-done.2 = bf16[4,16,3584]{2,1,0:T(8,128)(2,1)} collective-permute-done((bf16[4,16,3584]{2,1,0:T(8,128)(2,1)}, bf16[4,16,3584]{2,1,0:T(8,128)(2,1)}, u32[]{:S(2)}, u32[]{:S(2)}) %collective-permute-start.2) | collective-permute-done | bytes 458784 | tf_op jit(solution)/shard_map/ppermute | solution.py:15
  120.5 1.6 fusion.51
  122.1 0.5 multiply_reduce_fusion
  122.6 2.3 fusion.60
  124.9 1.6 gather_fusion.6
  126.5 0.9 select_select_fusion.1
  127.4 6.8 %all-to-all-start.3 = ((bf16[4,16,3584]{2,1,0:T(8,128)(2,1)}), bf16[4,16,3584]{2,1,0:T(8,128)(2,1)S(1)}, u32[]{:S(2)}, u32[]{:S(2)}) async-start(bf16[4,16,3584]{2,1,0:T(8,128)(2,1)} %select_select_fusion.1), calls=%async_computation.3 | async-start | bytes 917504 | tf_op jit(solution)/shard_map/all_to_all | solution.py:85
  134.5 10.0 %all-to-all-done.3 = bf16[4,16,3584]{2,1,0:T(8,128)(2,1)S(1)} async-done(((bf16[4,16,3584]{2,1,0:T(8,128)(2,1)}), bf16[4,16,3584]{2,1,0:T(8,128)(2,1)S(1)}, u32[]{:S(2)}, u32[]{:S(2)}) %all-to-all-start.3) | async-done | bytes 458784 | tf_op jit(solution)/shard_map/all_to_all | solution.py:85
  144.5 1.3 gather_fusion.7
  145.8 1.2 select_select_fusion
  147.0 1.9 collective-permute-start.3
  148.9 6.0 %collective-permute-done.3 = bf16[4,16,3584]{2,1,0:T(8,128)(2,1)S(1)} collective-permute-done((bf16[4,16,3584]{2,1,0:T(8,128)(2,1)S(1)}, bf16[4,16,3584]{2,1,0:T(8,128)(2,1)S(1)}, u32[]{:S(2)}, u32[]{:S(2)}) %collective-permute-start.3) | collective-permute-done | bytes 458784 | tf_op jit(solution)/shard_map/ppermute | solution.py:15
  154.9 0.6 fusion.48
  155.5 1.7 convolution_convert_fusion
  157.2 0.6 convolution_convert_fusion.1
  157.8 1.7 pad_maximum_fusion
  159.6 111.7 %all-reduce.4.cloned.1.call-done = bf16[3584,384]{0,1:T(8,128)(2,1)} async-done(((bf16[3584,384]{0,1:T(8,128)(2,1)}), bf16[3584,384]{0,1:T(8,128)(2,1)}) %all-reduce.4.cloned.1.call-update) | async-done | bytes 2752528 | tf_op jit(solution)/shard_map/psum | solution.py:164
  271.3 1.2 convert_convert_fusion
  272.4 0.9 slice_bitcast_fusion
  (85 shorter events, 3.4 us)
Async XLA Ops:
  7.2 5.7 %copy-start = (bf16[1,1,3584,192]{2,3,1,0:T(8,128)(2,1)S(1)}, bf16[1,1,3584,192]{2,3,1,0:T(8,128)(2,1)}, u32[]{:S(2)}) copy-start(bf16[1,1,3584,192]{2,3,1,0:T(8,128)(2,1)} %param.10) | copy-start | bytes 4128772
  10.6 3.9 %copy-start.3 = (bf16[1,1,4,16,3584]{4,3,2,1,0:T(8,128)(2,1)S(1)}, bf16[1,1,4,16,3584]{4,3,2,1,0:T(8,128)(2,1)}, u32[]{:S(2)}) copy-start(bf16[1,1,4,16,3584]{4,3,2,1,0:T(8,128)(2,1)} %param.8) | copy-start | bytes 1376260
  12.8 2.7 copy-start.1
  15.5 2.3 copy-start.11
  15.5 2.6 copy-start.10
  15.9 9.9 %collective-permute-start = (bf16[4,16,3584]{2,1,0:T(8,128)(2,1)S(1)}, bf16[4,16,3584]{2,1,0:T(8,128)(2,1)}, u32[]{:S(2)}, u32[]{:S(2)}) collective-permute-start(bf16[4,16,3584]{2,1,0:T(8,128)(2,1)S(1)} %bitcast.118), channel_id=1, source_target_pairs={{0,4},{4,8},{8,12},{12,16},{16,20},{20,24},{24,28},{1,5},{5,9},{9,... | collective-permute-start | bytes 1376264 | tf_op jit(solution)/shard_map/ppermute | solution.py:15
  28.3 14.2 %all-to-all-start = ((bf16[4,16,3584]{2,1,0:T(8,128)(2,1)}), bf16[4,16,3584]{2,1,0:T(8,128)(2,1)}, u32[]{:S(2)}, u32[]{:S(2)}) async-start(bf16[4,16,3584]{2,1,0:T(8,128)(2,1)} %select_select_fusion.7), calls=%async_computation | async-start | bytes 917504 | tf_op jit(solution)/shard_map/all_to_all | solution.py:68
  46.5 10.1 %collective-permute-start.1 = (bf16[4,16,3584]{2,1,0:T(8,128)(2,1)}, bf16[4,16,3584]{2,1,0:T(8,128)(2,1)}, u32[]{:S(2)}, u32[]{:S(2)}) collective-permute-start(bf16[4,16,3584]{2,1,0:T(8,128)(2,1)} %bitcast.10), channel_id=1, source_target_pairs={{0,4},{4,8},{8,12},{12,16},{16,20},{20,24},{24,28},{1,5},{5,9},{9,... | collective-permute-start | bytes 1376264 | tf_op jit(solution)/shard_map/ppermute | solution.py:15
  60.9 16.8 %all-to-all-start.1 = ((bf16[4,16,3584]{2,1,0:T(8,128)(2,1)}), bf16[4,16,3584]{2,1,0:T(8,128)(2,1)}, u32[]{:S(2)}, u32[]{:S(2)}) async-start(bf16[4,16,3584]{2,1,0:T(8,128)(2,1)} %select_select_fusion.5), calls=%async_computation.1 | async-start | bytes 917504 | tf_op jit(solution)/shard_map/all_to_all | solution.py:68
  81.6 1.9 copy-start.5
  83.4 1.0 copy-start.2
  84.5 1.0 copy-start.4
  91.2 16.8 %all-to-all-start.2 = ((bf16[4,16,3584]{2,1,0:T(8,128)(2,1)}), bf16[4,16,3584]{2,1,0:T(8,128)(2,1)}, u32[]{:S(2)}, u32[]{:S(2)}) async-start(bf16[4,16,3584]{2,1,0:T(8,128)(2,1)} %select_select_fusion.3), calls=%async_computation.2 | async-start | bytes 917504 | tf_op jit(solution)/shard_map/all_to_all | solution.py:85
  112.3 8.2 %collective-permute-start.2 = (bf16[4,16,3584]{2,1,0:T(8,128)(2,1)}, bf16[4,16,3584]{2,1,0:T(8,128)(2,1)}, u32[]{:S(2)}, u32[]{:S(2)}) collective-permute-start(bf16[4,16,3584]{2,1,0:T(8,128)(2,1)} %select_select_fusion.2), channel_id=1, source_target_pairs={{4,0},{8,4},{12,8},{16,12},{20,16},{24,20},{28,24},{5,1},{9,5},{13... | collective-permute-start | bytes 1376264 | tf_op jit(solution)/shard_map/ppermute | solution.py:15
  127.4 17.0 %all-to-all-start.3 = ((bf16[4,16,3584]{2,1,0:T(8,128)(2,1)}), bf16[4,16,3584]{2,1,0:T(8,128)(2,1)S(1)}, u32[]{:S(2)}, u32[]{:S(2)}) async-start(bf16[4,16,3584]{2,1,0:T(8,128)(2,1)} %select_select_fusion.1), calls=%async_computation.3 | async-start | bytes 917504 | tf_op jit(solution)/shard_map/all_to_all | solution.py:85
  134.2 137.0 %all-reduce.4.cloned.1.call-start = ((), (), s32[]{:S(2)}) async-start(), calls=%async_computation.4 | async-start | bytes 5505024 | tf_op jit(solution)/shard_map/psum | solution.py:164
  145.8 9.7 %copy-start.7 = (bf16[64,3584]{1,0:T(8,128)(2,1)S(1)}, bf16[64,3584]{1,0:T(8,128)(2,1)}, u32[]{:S(2)}) copy-start(bf16[64,3584]{1,0:T(8,128)(2,1)} %get-tuple-element.16) | copy-start | bytes 1376260
  147.0 7.9 %collective-permute-start.3 = (bf16[4,16,3584]{2,1,0:T(8,128)(2,1)S(1)}, bf16[4,16,3584]{2,1,0:T(8,128)(2,1)S(1)}, u32[]{:S(2)}, u32[]{:S(2)}) collective-permute-start(bf16[4,16,3584]{2,1,0:T(8,128)(2,1)S(1)} %select_select_fusion), channel_id=1, source_target_pairs={{4,0},{8,4},{12,8},{16,12},{20,16},{24,20},{28,24},{5,1},{9,5},{13... | collective-permute-start | bytes 1376264 | tf_op jit(solution)/shard_map/ppermute | solution.py:15
  155.5 1.7 copy-start.6
  155.5 1.7 copy-start.8
  155.5 1.7 copy-start.9
Sparse Core Ops, SparseCore 0:
  159.7 111.5 all-reduce.3
where the time goes:
time: 284 us; the launch traced here: 280 us
  waiting for transfers between devices  171 us (60%)
  starting transfers between devices  34.6 us (12%)
  other arithmetic  28.1 us (10%)
  local copies, waits for them, and re-layouts  21.3 us (8%)
  between operations  14.5 us (5%)
  matrix products  10.3 us (4%)
    psum x1, waiting for transfers between devices, local(): lax.psum(jnp.concatenate([reduce_rows, expand_rows], axis=1).astype(jnp.b...  112 us
    ppermute x4, waiting for transfers between devices, from_behind(): return lax.ppermute(block, axis, route)  24.8 us
    all_to_all x2, waiting for transfers between devices, homeward(): lax.all_to_all(parcel, 'rep', split_axis=0, concat_axis=0, tiled=True)  19.1 us
    all_to_all x2, waiting for transfers between devices, onward(): lax.all_to_all(bucket, 'rep', split_axis=0, concat_axis=0, tiled=True)  15.8 us
    gather x8, local copies, waits for them, and re-layouts, gather_slots(): picked = jnp.take(source, slot_index, axis=0)  15.6 us
    all_to_all x2, starting transfers between devices, homeward(): lax.all_to_all(parcel, 'rep', split_axis=0, concat_axis=0, tiled=True)  14.3 us
    all_to_all x2, starting transfers between devices, onward(): lax.all_to_all(bucket, 'rep', split_axis=0, concat_axis=0, tiled=True)  12.7 us
    select_n x6, other arithmetic, gather_slots(): return jnp.where(present[:, None, None], picked, jnp.zeros_like(picked))  8.75 us
  transfers between devices with their start and end apart: 9, of which 9 were waited for; matrix products, arithmetic and copies ran while one was open for 2% of the time, Pallas kernels for 0%

commit v1 on v0

v1 whole, which is shorter than its diff:
```python
import functools

import jax
import jax.numpy as jnp
from jax import lax
from jax.experimental import pallas as pl
from jax.experimental.pallas import tpu as pltpu
from jax.sharding import PartitionSpec as P

TICKS = 3
HOPS = TICKS - 1
EPS = 1e-06
MESH = pl.DeviceIdType.MESH
NT = (((1,), (1,)), ((), ()))
NN = (((1,), (0,)), ((), ()))


def dot(a, b, dims):
    return lax.dot_general(a, b, dims, preferred_element_type=jnp.float32)


def chunks(total, size):
    return [(start, min(size, total - start)) for start in range(0, total, size)]


def kernel(
    sections, n, cap, rows, features, rank,
    held, routes, inflow_hbm, cot_hbm, wr_hbm, we_hbm,
    out,
    inflow, cot, wr, we,
    lanes, landed0, landed1, fwd_out, bwd_out, back, ups, normed, inv, pre, hid, gp,
    part, up_buf, down_buf,
    load_sem, send_sem, recv_sem, bsend_sem, brecv_sem,
    up_send, up_recv, down_send, down_recv,
):
    c = lax.axis_index("section")
    r = lax.axis_index("rep")
    tick_rows = n * rows
    share = features // n
    column_chunks = chunks(features, 512)
    landed = (landed0, landed1)

    loads = [
        pltpu.make_async_copy(src, dst, load_sem.at[i])
        for i, (src, dst) in enumerate(
            [(inflow_hbm, inflow), (wr_hbm, wr), (we_hbm, we), (cot_hbm, cot)]
        )
    ]
    for load in loads:
        load.start()

    barrier = pltpu.get_barrier_semaphore()
    for step in (1, -1):
        other = c + step

        @pl.when((other >= 0) & (other < sections))
        def _():
            for d in range(n):
                pl.semaphore_signal(barrier, inc=1, device_id=(other, d), device_id_type=MESH)

        near = r + step

        @pl.when((near >= 0) & (near < n))
        def _():
            pl.semaphore_signal(barrier, inc=1, device_id=(c, near), device_id_type=MESH)

    def one_if(condition):
        return condition.astype(jnp.int32)

    pl.semaphore_wait(
        barrier,
        n * (one_if(c > 0) + one_if(c < sections - 1)) + one_if(r > 0) + one_if(r < n - 1),
    )

    prev = jnp.maximum(c - 1, 0)
    prev2 = jnp.maximum(c - 2, 0)
    zero = jnp.int32(0)

    def first_tick_sends(section, s, dest):
        def step(k, carry):
            slot, seen = carry
            hit = ((routes[0, section, s, k] == dest) & (k < held[section, s])).astype(jnp.int32)
            return slot + hit * k, seen + hit
        return lax.fori_loop(0, cap, step, (zero, zero), unroll=cap <= 4)

    lane0 = [first_tick_sends(c, r, d) for d in range(n)]
    sent0 = [
        first_tick_sends(prev, s, r)[1] * (c >= 1).astype(jnp.int32) for s in range(n)
    ]

    def ranks(sent):
        total, out_ranks = zero, []
        for s in range(n):
            out_ranks.append(total)
            total = total + sent[s]
        return out_ranks

    rank1 = [jnp.minimum(v, cap - 1) for v in ranks(sent0)]
    dest1 = [routes[1, c, r, rank1[s]] for s in range(n)]
    lane1 = []
    for d in range(n):
        index, seen = zero, zero
        for s in range(n):
            hit = sent0[s] * (dest1[s] == d).astype(jnp.int32)
            index, seen = index + hit * s, seen + hit
        lane1.append((index, seen))

    def count1(s):
        def step(s0, total):
            return total + first_tick_sends(prev2, s0, s)[1]
        return lax.fori_loop(0, n, step, zero, unroll=n <= 4) * (c >= 2).astype(jnp.int32)

    sent1 = []
    for s in range(n):
        count = count1(s)

        def step(k, seen, s=s, count=count):
            return seen + ((routes[1, prev, s, k] == r) & (k < count)).astype(jnp.int32)
        sent1.append(lax.fori_loop(0, cap, step, zero, unroll=cap <= 4))
    rank2 = [jnp.minimum(v, cap - 1) for v in ranks(sent1)]

    def pick(source, index, seen):
        value = source[pl.ds(index, 1)][0]
        return jnp.where(seen > 0, value, jnp.zeros_like(value))

    def live_at(tick, section):
        return (section >= tick) & (section <= sections - TICKS + tick)

    def hop_copies(hop, forward):
        buf = fwd_out if forward else bwd_out
        dst = landed[hop] if forward else ups.at[hop]
        sems = (send_sem, recv_sem) if forward else (bsend_sem, brecv_sem)
        target = c + 1 if forward else c - 1
        return [
            pltpu.make_async_remote_copy(
                src_ref=buf.at[hop, d],
                dst_ref=dst.at[r],
                send_sem=sems[0].at[hop, d],
                recv_sem=sems[1].at[hop, r],
                device_id=(target, d),
                device_id_type=MESH,
            )
            for d in range(n)
        ]

    def await_lanes(hop, forward):
        buf = fwd_out if forward else bwd_out
        dst = landed[hop] if forward else ups.at[hop]
        sems = (send_sem, recv_sem) if forward else (bsend_sem, brecv_sem)
        for s in range(n):
            pltpu.make_async_remote_copy(
                src_ref=buf.at[hop, s],
                dst_ref=dst.at[s],
                send_sem=sems[0].at[hop, s],
                recv_sem=sems[1].at[hop, s],
                device_id=(c, s),
                device_id_type=MESH,
            ).wait_recv()

    def normalise(tick, i, lane):
        lanes[tick, i] = lane
        wide = lane.astype(jnp.float32)
        scale = lax.rsqrt(jnp.mean(wide * wide, axis=-1, keepdims=True) + EPS)
        at = pl.ds(tick * tick_rows + i * rows, rows)
        inv[at, :] = jnp.broadcast_to(scale, (rows, 128))
        normed[at, :] = (wide * scale).astype(jnp.bfloat16)

    def forward(tick):
        at = pl.ds(tick * tick_rows, tick_rows)
        p = dot(normed[at, :], wr[...], NT)
        pre[at, :] = p
        h = (p / (1.0 + jnp.exp(-p))).astype(jnp.bfloat16)
        hid[at, :] = h
        return h

    def emit(tick, h):
        for start, size in column_chunks:
            cols = pl.ds(start, size)
            branch = dot(h, we[:, cols], NN).reshape(n, rows, size)
            fwd_out[tick, :, :, cols] = (
                lanes[tick, :, :, cols].astype(jnp.float32) + branch
            ).astype(jnp.bfloat16)

        @pl.when(live_at(tick, c))
        def _():
            for copy in hop_copies(tick, True):
                copy.start()

    def receive(hop, forward, tick):
        dst = landed[hop] if forward else ups.at[hop]

        @pl.when(live_at(tick, c))
        def _():
            await_lanes(hop, forward)

        @pl.when(jnp.logical_not(live_at(tick, c)))
        def _():
            dst[...] = jnp.zeros(dst.shape, dst.dtype)

    loads[0].wait()
    for d in range(n):
        normalise(0, d, pick(inflow, *lane0[d]))
    loads[1].wait()
    h = forward(0)
    loads[2].wait()
    emit(0, h)
    loads[3].wait()
    for s in range(n):
        ups[2, s] = pick(cot, rank2[s], sent1[s])

    receive(0, True, 1)
    for d in range(n):
        normalise(1, d, pick(landed0, *lane1[d]))
    emit(1, forward(1))

    receive(1, True, 2)
    for s in range(n):
        normalise(2, s, landed1[s])
    forward(2)

    def backward(tick):
        at = pl.ds(tick * tick_rows, tick_rows)
        grad_hidden = dot(ups[tick].reshape(tick_rows, features), we[...], NT)
        p = pre[at, :]
        sig = 1.0 / (1.0 + jnp.exp(-p))
        g = (grad_hidden * sig * (1.0 + p * (1.0 - sig))).astype(jnp.bfloat16)
        gp[at, :] = g
        if tick == 0:
            return
        inner = jnp.sum(g.astype(jnp.float32) * p, axis=-1, keepdims=True) * (1.0 / features)
        scale = inv[at, :][:, :1]
        for start, size in column_chunks:
            cols = pl.ds(start, size)
            grad_unit = dot(g, wr[:, cols], NN)
            unit = lanes[tick, :, :, cols].astype(jnp.float32).reshape(tick_rows, size) * scale
            up = ups[tick, :, :, cols].astype(jnp.float32).reshape(tick_rows, size)
            value = up + scale * (grad_unit - unit * inner)
            value = value.astype(jnp.bfloat16).reshape(n, rows, size)
            if tick == 2:
                bwd_out[1, :, :, cols] = value
            else:
                back[:, :, cols] = value
        if tick == 1:
            for s in range(n):
                bwd_out[0, s] = pick(back, dest1[s], sent0[s])

        @pl.when(live_at(tick, c))
        def _():
            for copy in hop_copies(tick - 1, False):
                copy.start()

    backward(2)
    receive(1, False, 1)
    backward(1)
    receive(0, False, 0)
    backward(0)

    left = [gp[...], hid[...]]
    left = [v.astype(jnp.float32).T.astype(jnp.bfloat16) for v in left]
    for q in range(n):
        cols = pl.ds(q * share, share)
        part[q, 0] = dot(left[0], normed[:, cols], NN).astype(jnp.bfloat16)
        right = ups[:, :, :, cols].reshape(TICKS * tick_rows, share)
        part[q, 1] = dot(left[1], right, NN).astype(jnp.bfloat16)

    def chain(buf, sems, q, m, to):
        return pltpu.make_async_remote_copy(
            src_ref=buf.at[q, m],
            dst_ref=buf.at[q, m],
            send_sem=sems[0].at[q, m],
            recv_sem=sems[1].at[q, m],
            device_id=(c, to),
            device_id_type=MESH,
        )

    flows = [
        (up_buf, (up_send, up_recv), r, 1),
        (down_buf, (down_send, down_recv), n - 1 - r, -1),
    ]
    for slot in range(n - 1):
        for m in range(2):
            for buf, sems, distance, direction in flows:
                late = slot - distance

                @pl.when(late >= 0)
                def _():
                    q = n - 1 - late if direction > 0 else late
                    copy = chain(buf, sems, q, m, r + direction)

                    @pl.when(distance == 0)
                    def _():
                        buf[q, m] = part[q, m]

                    @pl.when(distance > 0)
                    def _():
                        copy.wait_recv()
                        buf[q, m] = (
                            buf[q, m].astype(jnp.float32) + part[q, m].astype(jnp.float32)
                        ).astype(jnp.bfloat16)

                    copy.start()

    for m in range(2):
        @pl.when(r == 0)
        def _():
            chain(down_buf, (down_send, down_recv), r, m, r).wait_recv()
            out[m, 0] = (
                part[r, m].astype(jnp.float32) + down_buf[r, m].astype(jnp.float32)
            ).astype(jnp.bfloat16)

        @pl.when(r == n - 1)
        def _():
            chain(up_buf, (up_send, up_recv), r, m, r).wait_recv()
            out[m, 0] = (
                part[r, m].astype(jnp.float32) + up_buf[r, m].astype(jnp.float32)
            ).astype(jnp.bfloat16)

        @pl.when((r > 0) & (r < n - 1))
        def _():
            chain(down_buf, (down_send, down_recv), r, m, r).wait_recv()
            chain(up_buf, (up_send, up_recv), r, m, r).wait_recv()
            out[m, 0] = (
                part[r, m].astype(jnp.float32)
                + down_buf[r, m].astype(jnp.float32)
                + up_buf[r, m].astype(jnp.float32)
            ).astype(jnp.bfloat16)

    for slot in range(n - 1):
        for m in range(2):
            for buf, sems, distance, direction in flows:
                late = slot - distance

                @pl.when(late >= 0)
                def _():
                    q = n - 1 - late if direction > 0 else late
                    chain(buf, sems, q, m, r + direction).wait_send()
    for hop in range(HOPS):
        @pl.when(live_at(hop, c))
        def _():
            for copy in hop_copies(hop, True):
                copy.wait_send()

        @pl.when(live_at(hop + 1, c))
        def _():
            for copy in hop_copies(hop, False):
                copy.wait_send()


def local(sections, n, inflow, cotangent, reduce_weight, expand_weight, held, routes):
    cap, rows, features = inflow.shape[2:]
    rank = reduce_weight.shape[3]
    share = features // n
    total = TICKS * n * rows
    bf16, f32 = jnp.bfloat16, jnp.float32
    dma = pltpu.SemaphoreType.DMA
    smem = pl.BlockSpec(memory_space=pltpu.SMEM)
    anywhere = pl.BlockSpec(memory_space=pl.ANY)
    lane_set = (n, rows, features)
    grads = pl.pallas_call(
        functools.partial(kernel, sections, n, cap, rows, features, rank),
        out_shape=jax.ShapeDtypeStruct((2, 1, rank, share), bf16),
        in_specs=[smem, smem, anywhere, anywhere, anywhere, anywhere],
        out_specs=pl.BlockSpec(memory_space=pltpu.VMEM),
        scratch_shapes=[
            pltpu.VMEM((cap, rows, features), bf16),
            pltpu.VMEM((cap, rows, features), bf16),
            pltpu.VMEM((rank, features), bf16),
            pltpu.VMEM((rank, features), bf16),
            pltpu.VMEM((TICKS,) + lane_set, bf16),
            pltpu.VMEM(lane_set, bf16),
            pltpu.VMEM(lane_set, bf16),
            pltpu.VMEM((HOPS,) + lane_set, bf16),
            pltpu.VMEM((HOPS,) + lane_set, bf16),
            pltpu.VMEM(lane_set, bf16),
            pltpu.VMEM((TICKS,) + lane_set, bf16),
            pltpu.VMEM((total, features), bf16),
            pltpu.VMEM((total, 128), f32),
            pltpu.VMEM((total, rank), f32),
            pltpu.VMEM((total, rank), bf16),
            pltpu.VMEM((total, rank), bf16),
            pltpu.VMEM((n, 2, rank, share), bf16),
            pltpu.VMEM((n, 2, rank, share), bf16),
            pltpu.VMEM((n, 2, rank, share), bf16),
            dma((4,)),
            dma((HOPS, n)), dma((HOPS, n)), dma((HOPS, n)), dma((HOPS, n)),
            dma((n, 2)), dma((n, 2)), dma((n, 2)), dma((n, 2)),
        ],
        compiler_params=pltpu.CompilerParams(
            collective_id=0, has_side_effects=True, vmem_limit_bytes=56 * 1024 * 1024
        ),
    )(
        held,
        routes,
        inflow[0, 0],
        cotangent[0, 0],
        jnp.swapaxes(reduce_weight[0, 0], 0, 1),
        jnp.swapaxes(expand_weight[0, 0], 0, 1),
    )
    return (jnp.swapaxes(grads[0], 1, 2), jnp.swapaxes(grads[1], 1, 2))


def solution(mesh):
    placed = (
        P("section", "rep", None, None, None),
        P("section", "rep", None, None, None),
        P("section", "rep", None, None),
        P("section", "rep", None, None),
        P(),
        P(),
    )
    return jax.shard_map(
        functools.partial(local, mesh.shape["section"], mesh.shape["rep"]),
        mesh=mesh,
        in_specs=placed,
        out_specs=(P("section", "rep", None), P("section", "rep", None)),
        check_vma=False,
    )
```

time: 284 us -> 109 us (0.38); the launches traced: 280 us -> 109 us
  waiting for transfers between devices: 171 us -> 0 us
  Pallas kernels: 0 us -> 103 us
  starting transfers between devices: 34.6 us -> 0 us
  other arithmetic: 28.1 us -> 0 us
  local copies, waits for them, and re-layouts: 21.3 us -> 4.78 us
  between operations: 14.5 us -> 0.64 us
  matrix products: 10.3 us -> 0 us
    psum x1 -> x0, waiting for transfers between devices: 112 us -> none  [local(): lax.psum(jnp.concatenate([reduce_rows, expand_rows], axis=1).astype(jnp.b...]
    pallas_call x0 -> x1, Pallas kernels: none -> 103 us  [local(): pl.pallas_call(functools.partial(kernel, sections, n, cap, rows, features...]
    all_to_all x4 -> x0, waiting for transfers between devices: 34.9 us -> none  [the longest x2 19.1 us: homeward(): lax.all_to_all(parcel, 'rep', split_axis=0, concat_axis=0, tiled=True)]
    all_to_all x4 -> x0, starting transfers between devices: 27 us -> none  [the longest x2 14.3 us: homeward(): lax.all_to_all(parcel, 'rep', split_axis=0, concat_axis=0, tiled=True)]
    ppermute x4 -> x0, waiting for transfers between devices: 24.8 us -> none  [from_behind(): return lax.ppermute(block, axis, route)]
    gather x8 -> x0, local copies, waits for them, and re-layouts: 15.6 us -> none  [gather_slots(): picked = jnp.take(source, slot_index, axis=0)]
    select_n x15 -> x0, other arithmetic: 10.7 us -> none  [the longest x6 8.75 us: gather_slots(): return jnp.where(present[:, None, None], picked, jnp.zeros_like(picked))]
    dot_general x12 -> x0, matrix products: 10.3 us -> none  [the longest x3 2.82 us: layer_parts(): pre_act = jnp.dot(normed, reduce_w, preferred_element_type=jnp.float32)]
  transfers between devices with their start and end apart: 9 -> 0, of which waited for: 9 -> 0; matrix products, arithmetic and copies ran while one was open for 2% -> 0% of each run, Pallas kernels for 0% -> 0%
where the time goes in v1:
time: 109 us
  Pallas kernels  103 us (94%)
  local copies, waits for them, and re-layouts  4.78 us (4%)
    pallas_call x1, Pallas kernels, local(): pl.pallas_call(functools.partial(kernel, sections, n, cap, rows, features...  103 us
    unnamed x2, local copies, waits for them, and re-layouts  2.79 us

profile of v1, /device:TPU:18, one launch (start us, length us, event | category | flops | bytes accessed | tf_op | source)
XLA Modules:
  0.0 108.7 jit_solution(10788240393661566960)
XLA Ops:
  0.6 1.3 %copy.8.held = s32[8,4]{1,0:T(8,128)} copy(s32[8,4]{0,1:T(4,128)} %param.10) | data formatting | bytes 256 | tf_op args[4]
  2.0 1.4 %copy.9.routes = s32[2,8,4,4]{3,2,1,0:T(4,128)} copy(s32[2,8,4,4]{1,3,2,0:T(4,128)} %param.11) | data formatting | bytes 2048 | tf_op args[5]
  3.4 103.3 %shard_map.77 = bf16[2,1,192,896]{3,2,1,0:T(8,128)(2,1)} custom-call(s32[8,4]{1,0:T(8,128)} %copy.8.held, s32[2,8,4,4]{3,2,1,0:T(4,128)} %copy.9.routes, bf16[4,16,3584]{2,1,0:T(8,128)(2,1)} %bitcast.18, bf16[4,16,3584]{2,1,0:T(8,128)(2,1)} %bitcast.19, bf16[192,3584]{1,0:T(8,128)(2,1)} %bitcast.16, bf16[192,3584]{1,0:T(8,128)(2,1)} %bitcast.17), custom_call_target="tpu_custom_call" | custom-call | tf_op jit(solution)/shard_map/pallas_call | solution.py:359
  106.7 2.0 %slice_bitcast_fusion = (bf16[1,896,192]{1,2,0:T(8,128)(2,1)}, bf16[1,896,192]{1,2,0:T(8,128)(2,1)}) fusion(bf16[2,1,192,896]{3,2,1,0:T(8,128)(2,1)} %shard_map.77), kind=kLoop, calls=%fused_computation | loop fusion | bytes 1376256 | tf_op jit(solution)/shard_map/transpose | solution.py:399

commit v2 on v1

--- a/solution.py
+++ b/solution.py
@@ -9,6 +9,7 @@
 
 TICKS = 3
 HOPS = TICKS - 1
+HALVES = 2
 EPS = 1e-06
 MESH = pl.DeviceIdType.MESH
 NT = (((1,), (1,)), ((), ()))
@@ -37,7 +38,11 @@
     r = lax.axis_index("rep")
     tick_rows = n * rows
     share = features // n
-    column_chunks = chunks(features, 512)
+    half = features // HALVES
+    halves = [
+        (pl.ds(h * half, half), [(h * half + a, b) for a, b in chunks(half, 896)])
+        for h in range(HALVES)
+    ]
     landed = (landed0, landed1)
 
     loads = [
@@ -126,33 +131,33 @@
     def live_at(tick, section):
         return (section >= tick) & (section <= sections - TICKS + tick)
 
-    def hop_copies(hop, forward):
+    def hop_copies(hop, forward, h):
         buf = fwd_out if forward else bwd_out
         dst = landed[hop] if forward else ups.at[hop]
         sems = (send_sem, recv_sem) if forward else (bsend_sem, brecv_sem)
         target = c + 1 if forward else c - 1
         return [
             pltpu.make_async_remote_copy(
-                src_ref=buf.at[hop, d],
-                dst_ref=dst.at[r],
-                send_sem=sems[0].at[hop, d],
-                recv_sem=sems[1].at[hop, r],
+                src_ref=buf.at[hop, d, :, halves[h][0]],
+                dst_ref=dst.at[r, :, halves[h][0]],
+                send_sem=sems[0].at[hop, d, h],
+                recv_sem=sems[1].at[hop, r, h],
                 device_id=(target, d),
                 device_id_type=MESH,
             )
             for d in range(n)
         ]
 
-    def await_lanes(hop, forward):
+    def await_lane(hop, forward, s):
         buf = fwd_out if forward else bwd_out
         dst = landed[hop] if forward else ups.at[hop]
         sems = (send_sem, recv_sem) if forward else (bsend_sem, brecv_sem)
-        for s in range(n):
+        for h in range(HALVES):
             pltpu.make_async_remote_copy(
-                src_ref=buf.at[hop, s],
-                dst_ref=dst.at[s],
-                send_sem=sems[0].at[hop, s],
-                recv_sem=sems[1].at[hop, s],
+                src_ref=buf.at[hop, s, :, halves[h][0]],
+                dst_ref=dst.at[s, :, halves[h][0]],
+                send_sem=sems[0].at[hop, s, h],
+                recv_sem=sems[1].at[hop, s, h],
                 device_id=(c, s),
                 device_id_type=MESH,
             ).wait_recv()
@@ -173,29 +178,34 @@
         hid[at, :] = h
         return h
 
-    def emit(tick, h):
-        for start, size in column_chunks:
-            cols = pl.ds(start, size)
-            branch = dot(h, we[:, cols], NN).reshape(n, rows, size)
-            fwd_out[tick, :, :, cols] = (
-                lanes[tick, :, :, cols].astype(jnp.float32) + branch
-            ).astype(jnp.bfloat16)
+    def emit(tick, hidden):
+        for h, (_, parts) in enumerate(halves):
+            for start, size in parts:
+                cols = pl.ds(start, size)
+                branch = dot(hidden, we[:, cols], NN).reshape(n, rows, size)
+                fwd_out[tick, :, :, cols] = (
+                    lanes[tick, :, :, cols].astype(jnp.float32) + branch
+                ).astype(jnp.bfloat16)
+
+            @pl.when(live_at(tick, c))
+            def _():
+                for copy in hop_copies(tick, True, h):
+                    copy.start()
+
+    def receive(hop, forward, tick, s):
+        dst = landed[hop] if forward else ups.at[hop]
 
         @pl.when(live_at(tick, c))
         def _():
-            for copy in hop_copies(tick, True):
-                copy.start()
-
-    def receive(hop, forward, tick):
-        dst = landed[hop] if forward else ups.at[hop]
-
-        @pl.when(live_at(tick, c))
-        def _():
-            await_lanes(hop, forward)
+            await_lane(hop, forward, s)
 
         @pl.when(jnp.logical_not(live_at(tick, c)))
         def _():
-            dst[...] = jnp.zeros(dst.shape, dst.dtype)
+            dst[s] = jnp.zeros(dst.shape[1:], dst.dtype)
+
+    def receive_all(hop, forward, tick):
+        for s in range(n):
+            receive(hop, forward, tick, s)
 
     loads[0].wait()
     for d in range(n):
@@ -208,13 +218,13 @@
     for s in range(n):
         ups[2, s] = pick(cot, rank2[s], sent1[s])
 
-    receive(0, True, 1)
+    receive_all(0, True, 1)
     for d in range(n):
         normalise(1, d, pick(landed0, *lane1[d]))
     emit(1, forward(1))
 
-    receive(1, True, 2)
     for s in range(n):
+        receive(1, True, 2, s)
         normalise(2, s, landed1[s])
     forward(2)
 
@@ -229,43 +239,41 @@
             return
         inner = jnp.sum(g.astype(jnp.float32) * p, axis=-1, keepdims=True) * (1.0 / features)
         scale = inv[at, :][:, :1]
-        for start, size in column_chunks:
-            cols = pl.ds(start, size)
-            grad_unit = dot(g, wr[:, cols], NN)
-            unit = lanes[tick, :, :, cols].astype(jnp.float32).reshape(tick_rows, size) * scale
-            up = ups[tick, :, :, cols].astype(jnp.float32).reshape(tick_rows, size)
-            value = up + scale * (grad_unit - unit * inner)
-            value = value.astype(jnp.bfloat16).reshape(n, rows, size)
-            if tick == 2:
-                bwd_out[1, :, :, cols] = value
-            else:
-                back[:, :, cols] = value
-        if tick == 1:
-            for s in range(n):
-                bwd_out[0, s] = pick(back, dest1[s], sent0[s])
-
-        @pl.when(live_at(tick, c))
-        def _():
-            for copy in hop_copies(tick - 1, False):
-                copy.start()
+        for h, (half_cols, parts) in enumerate(halves):
+            for start, size in parts:
+                cols = pl.ds(start, size)
+                grad_unit = dot(g, wr[:, cols], NN)
+                unit = lanes[tick, :, :, cols].astype(jnp.float32).reshape(tick_rows, size) * scale
+                up = ups[tick, :, :, cols].astype(jnp.float32).reshape(tick_rows, size)
+                value = up + scale * (grad_unit - unit * inner)
+                value = value.astype(jnp.bfloat16).reshape(n, rows, size)
+                if tick == 2:
+                    bwd_out[1, :, :, cols] = value
+                else:
+                    back[:, :, cols] = value
+            if tick == 1:
+                for s in range(n):
+                    value = back[pl.ds(dest1[s], 1), :, half_cols][0]
+                    bwd_out[0, s, :, half_cols] = jnp.where(
+                        sent0[s] > 0, value, jnp.zeros_like(value)
+                    )
+
+            @pl.when(live_at(tick, c))
+            def _():
+                for copy in hop_copies(tick - 1, False, h):
+                    copy.start()
 
     backward(2)
-    receive(1, False, 1)
+    receive_all(1, False, 1)
     backward(1)
-    receive(0, False, 0)
+    receive_all(0, False, 0)
     backward(0)
 
     left = [gp[...], hid[...]]
     left = [v.astype(jnp.float32).T.astype(jnp.bfloat16) for v in left]
-    for q in range(n):
-        cols = pl.ds(q * share, share)
-        part[q, 0] = dot(left[0], normed[:, cols], NN).astype(jnp.bfloat16)
-        right = ups[:, :, :, cols].reshape(TICKS * tick_rows, share)
-        part[q, 1] = dot(left[1], right, NN).astype(jnp.bfloat16)
-
-    def chain(buf, sems, q, m, to):
+    def chain(buf, sems, q, m, to, first=False):
         return pltpu.make_async_remote_copy(
-            src_ref=buf.at[q, m],
+            src_ref=(part if first else buf).at[q, m],
             dst_ref=buf.at[q, m],
             send_sem=sems[0].at[q, m],
             recv_sem=sems[1].at[q, m],
@@ -277,27 +285,44 @@
         (up_buf, (up_send, up_recv), r, 1),
         (down_buf, (down_send, down_recv), n - 1 - r, -1),
     ]
-    for slot in range(n - 1):
+
+    def make_part(q, m):
+        cols = pl.ds(q * share, share)
+        if m == 0:
+            right = normed[:, cols]
+        else:
+            right = ups[:, :, :, cols].reshape(TICKS * tick_rows, share)
+        part[q, m] = dot(left[m], right, NN).astype(jnp.bfloat16)
+
+    for m in range(2):
+        for q, (buf, sems, distance, direction) in zip((n - 1, 0), flows):
+            make_part(q, m)
+
+            @pl.when(distance == 0)
+            def _():
+                chain(buf, sems, q, m, r + direction, True).start()
+
+    for q in range(n - 2, 0, -1):
+        for m in range(2):
+            make_part(q, m)
+
+    for slot in range(1, n - 1):
         for m in range(2):
             for buf, sems, distance, direction in flows:
                 late = slot - distance
-
-                @pl.when(late >= 0)
+                q = n - 1 - late if direction > 0 else late
+
+                @pl.when(distance == 0)
                 def _():
-                    q = n - 1 - late if direction > 0 else late
+                    chain(buf, sems, q, m, r + direction, True).start()
+
+                @pl.when((late >= 0) & (distance > 0))
+                def _():
                     copy = chain(buf, sems, q, m, r + direction)
-
-                    @pl.when(distance == 0)
-                    def _():
-                        buf[q, m] = part[q, m]
-
-                    @pl.when(distance > 0)
-                    def _():
-                        copy.wait_recv()
-                        buf[q, m] = (
-                            buf[q, m].astype(jnp.float32) + part[q, m].astype(jnp.float32)
-                        ).astype(jnp.bfloat16)
-
+                    copy.wait_recv()
+                    buf[q, m] = (
+                        buf[q, m].astype(jnp.float32) + part[q, m].astype(jnp.float32)
+                    ).astype(jnp.bfloat16)
                     copy.start()
 
     for m in range(2):
@@ -337,13 +362,15 @@
     for hop in range(HOPS):
         @pl.when(live_at(hop, c))
         def _():
-            for copy in hop_copies(hop, True):
-                copy.wait_send()
+            for h in range(HALVES):
+                for copy in hop_copies(hop, True, h):
+                    copy.wait_send()
 
         @pl.when(live_at(hop + 1, c))
         def _():
-            for copy in hop_copies(hop, False):
-                copy.wait_send()
+            for h in range(HALVES):
+                for copy in hop_copies(hop, False, h):
+                    copy.wait_send()
 
 
 def local(sections, n, inflow, cotangent, reduce_weight, expand_weight, held, routes):
@@ -382,7 +409,7 @@
             pltpu.VMEM((n, 2, rank, share), bf16),
             pltpu.VMEM((n, 2, rank, share), bf16),
             dma((4,)),
-            dma((HOPS, n)), dma((HOPS, n)), dma((HOPS, n)), dma((HOPS, n)),
+            dma((HOPS, n, HALVES)), dma((HOPS, n, HALVES)), dma((HOPS, n, HALVES)), dma((HOPS, n, HALVES)),
             dma((n, 2)), dma((n, 2)), dma((n, 2)), dma((n, 2)),
         ],
         compiler_params=pltpu.CompilerParams(

time: 109 us -> 110 us (level)
  Pallas kernels: 103 us -> 105 us
    pallas_call x1, Pallas kernels: 103 us -> 105 us  [local(): pl.pallas_call(functools.partial(kernel, sections, n, cap, rows, features...]
where the time goes in v2:
time: 110 us
  Pallas kernels  105 us (95%)
  local copies, waits for them, and re-layouts  4.78 us (4%)
    pallas_call x1, Pallas kernels, local(): pl.pallas_call(functools.partial(kernel, sections, n, cap, rows, features...  105 us
    unnamed x2, local copies, waits for them, and re-layouts  2.79 us

profile of v2, /device:TPU:18, one launch (start us, length us, event | category | flops | bytes accessed | tf_op | source)
XLA Modules:
  0.0 110.1 jit_solution(15833039056639103505)
XLA Ops:
  0.6 1.3 %copy.8.held = s32[8,4]{1,0:T(8,128)} copy(s32[8,4]{0,1:T(4,128)} %param.10) | data formatting | bytes 256 | tf_op args[4]
  2.0 1.4 %copy.9.routes = s32[2,8,4,4]{3,2,1,0:T(4,128)} copy(s32[2,8,4,4]{1,3,2,0:T(4,128)} %param.11) | data formatting | bytes 2048 | tf_op args[5]
  3.4 104.7 %shard_map.77 = bf16[2,1,192,896]{3,2,1,0:T(8,128)(2,1)} custom-call(s32[8,4]{1,0:T(8,128)} %copy.8.held, s32[2,8,4,4]{3,2,1,0:T(4,128)} %copy.9.routes, bf16[4,16,3584]{2,1,0:T(8,128)(2,1)} %bitcast.18, bf16[4,16,3584]{2,1,0:T(8,128)(2,1)} %bitcast.19, bf16[192,3584]{1,0:T(8,128)(2,1)} %bitcast.16, bf16[192,3584]{1,0:T(8,128)(2,1)} %bitcast.17), custom_call_target="tpu_custom_call" | custom-call | tf_op jit(solution)/shard_map/pallas_call | solution.py:386
  108.1 2.0 %slice_bitcast_fusion = (bf16[1,896,192]{1,2,0:T(8,128)(2,1)}, bf16[1,896,192]{1,2,0:T(8,128)(2,1)}) fusion(bf16[2,1,192,896]{3,2,1,0:T(8,128)(2,1)} %shard_map.77), kind=kLoop, calls=%fused_computation | loop fusion | bytes 1376256 | tf_op jit(solution)/shard_map/transpose | solution.py:426

commit v3 on v2

--- a/solution.py
+++ b/solution.py
@@ -128,6 +128,8 @@
         value = source[pl.ds(index, 1)][0]
         return jnp.where(seen > 0, value, jnp.zeros_like(value))
 
+    order = [lax.rem(r + (n // 2 + j) % n, n) for j in range(n) if (n // 2 + j) % n] + [r]
+
     def live_at(tick, section):
         return (section >= tick) & (section <= sections - TICKS + tick)
 
@@ -145,7 +147,7 @@
                 device_id=(target, d),
                 device_id_type=MESH,
             )
-            for d in range(n)
+            for d in order
         ]
 
     def await_lane(hop, forward, s):

time: 110 us -> 109 us (level); the launches traced: 110 us -> 107 us
  Pallas kernels: 105 us -> 101 us
    pallas_call x1, Pallas kernels: 105 us -> 101 us  [local(): pl.pallas_call(functools.partial(kernel, sections, n, cap, rows, features...]
where the time goes in v3:
time: 109 us; the launch traced here: 107 us
  Pallas kernels  101 us (93%)
  local copies, waits for them, and re-layouts  4.78 us (4%)
    pallas_call x1, Pallas kernels, local(): pl.pallas_call(functools.partial(kernel, sections, n, cap, rows, features...  101 us
    unnamed x2, local copies, waits for them, and re-layouts  2.79 us

profile of v3, /device:TPU:18, one launch (start us, length us, event | category | flops | bytes accessed | tf_op | source)
XLA Modules:
  0.0 106.6 jit_solution(4009465825553615140)
XLA Ops:
  0.6 1.3 %copy.8.held = s32[8,4]{1,0:T(8,128)} copy(s32[8,4]{0,1:T(4,128)} %param.10) | data formatting | bytes 256 | tf_op args[4]
  2.0 1.4 %copy.9.routes = s32[2,8,4,4]{3,2,1,0:T(4,128)} copy(s32[2,8,4,4]{1,3,2,0:T(4,128)} %param.11) | data formatting | bytes 2048 | tf_op args[5]
  3.4 101.2 %shard_map.77 = bf16[2,1,192,896]{3,2,1,0:T(8,128)(2,1)} custom-call(s32[8,4]{1,0:T(8,128)} %copy.8.held, s32[2,8,4,4]{3,2,1,0:T(4,128)} %copy.9.routes, bf16[4,16,3584]{2,1,0:T(8,128)(2,1)} %bitcast.18, bf16[4,16,3584]{2,1,0:T(8,128)(2,1)} %bitcast.19, bf16[192,3584]{1,0:T(8,128)(2,1)} %bitcast.16, bf16[192,3584]{1,0:T(8,128)(2,1)} %bitcast.17), custom_call_target="tpu_custom_call" | custom-call | tf_op jit(solution)/shard_map/pallas_call | solution.py:388
  104.7 2.0 %slice_bitcast_fusion = (bf16[1,896,192]{1,2,0:T(8,128)(2,1)}, bf16[1,896,192]{1,2,0:T(8,128)(2,1)}) fusion(bf16[2,1,192,896]{3,2,1,0:T(8,128)(2,1)} %shard_map.77), kind=kLoop, calls=%fused_computation | loop fusion | bytes 1376256 | tf_op jit(solution)/shard_map/transpose | solution.py:428

commit v4 on v3

--- a/solution.py
+++ b/solution.py
@@ -9,7 +9,7 @@
 
 TICKS = 3
 HOPS = TICKS - 1
-HALVES = 2
+HALVES = 1
 EPS = 1e-06
 MESH = pl.DeviceIdType.MESH
 NT = (((1,), (1,)), ((), ()))

time: 109 us -> 107 us (0.982); the launches traced: 107 us -> 106 us
  no operation moved by 1% of the time
where the time goes in v4:
time: 107 us; the launch traced here: 106 us
  Pallas kernels  100 us (93%)
  local copies, waits for them, and re-layouts  4.78 us (4%)
    pallas_call x1, Pallas kernels, local(): pl.pallas_call(functools.partial(kernel, sections, n, cap, rows, features...  100 us
    unnamed x2, local copies, waits for them, and re-layouts  2.79 us

profile of v4, /device:TPU:18, one launch (start us, length us, event | category | flops | bytes accessed | tf_op | source)
XLA Modules:
  0.0 105.8 jit_solution(3854043878118786044)
XLA Ops:
  0.6 1.3 %copy.8.held = s32[8,4]{1,0:T(8,128)} copy(s32[8,4]{0,1:T(4,128)} %param.10) | data formatting | bytes 256 | tf_op args[4]
  2.0 1.4 %copy.9.routes = s32[2,8,4,4]{3,2,1,0:T(4,128)} copy(s32[2,8,4,4]{1,3,2,0:T(4,128)} %param.11) | data formatting | bytes 2048 | tf_op args[5]
  3.4 100.4 %shard_map.77 = bf16[2,1,192,896]{3,2,1,0:T(8,128)(2,1)} custom-call(s32[8,4]{1,0:T(8,128)} %copy.8.held, s32[2,8,4,4]{3,2,1,0:T(4,128)} %copy.9.routes, bf16[4,16,3584]{2,1,0:T(8,128)(2,1)} %bitcast.18, bf16[4,16,3584]{2,1,0:T(8,128)(2,1)} %bitcast.19, bf16[192,3584]{1,0:T(8,128)(2,1)} %bitcast.16, bf16[192,3584]{1,0:T(8,128)(2,1)} %bitcast.17), custom_call_target="tpu_custom_call" | custom-call | tf_op jit(solution)/shard_map/pallas_call | solution.py:388
  103.8 2.0 %slice_bitcast_fusion = (bf16[1,896,192]{1,2,0:T(8,128)(2,1)}, bf16[1,896,192]{1,2,0:T(8,128)(2,1)}) fusion(bf16[2,1,192,896]{3,2,1,0:T(8,128)(2,1)} %shard_map.77), kind=kLoop, calls=%fused_computation | loop fusion | bytes 1376256 | tf_op jit(solution)/shard_map/transpose | solution.py:428
